TPU v7x, 32 devices: a whole 2x2x4 slice. The times are simulated.
32 devices in a mesh: rep: 8 (over z, y), fsdp: 4 (over x, core).
Axes of the slice: x: 2, y: 2, z: 4, core: 2. Of those that a mesh axis runs over, the one named last changes fastest.
Arguments:
- weights: bfloat16 [8, 4, 1024, 512], P('rep', None, 'fsdp'), may hold values from -6 to 6
- momentum: bfloat16 [8, 4, 1024, 512], P('rep', None, 'fsdp')
- gradient: bfloat16 [8, 4, 1024, 512], P('rep', None, 'fsdp')
- partner: int32 [8], replicated, may hold values from 0 to 7, as said below
Outputs:
- averaged: bfloat16 [8, 4, 1024, 512], P('rep', None, 'fsdp')
Inputs may be any that keep to these rules, and one draw needn't show every extreme that they name: partner[partner[r]] = r for every replica r, and partner[r] differs from r in exactly one bit of its binary index.
All inputs are finite; a program needn't handle non-finite values.
Results may differ from a plain program's by a relative error of at most 0.014.
Values may be sent and summed in bfloat16 or wider, within the bound.
A program may use at most 64 MiB of HBM per device.

v0:
```python
import functools
import math

import jax
import jax.numpy as jnp
from jax import lax
from jax.experimental import pallas as pl
from jax.experimental.pallas import tpu as pltpu
from jax.sharding import PartitionSpec as P

ITERS = 5

beta_moment = 0.95
epsilon_norm = 1e-07
coef_first = 3.4445
coef_second = -4.775
coef_third = 2.0315
learn_rate = 1.0
decay_rate = 0.1

MESH = pl.DeviceIdType.MESH
BF16, F32 = jnp.bfloat16, jnp.float32


def swapped(value, axis, distance):
    mask = 2**distance
    pairs = [(source, source ^ mask) for source in range(lax.axis_size(axis))]
    return lax.ppermute(value, axis, pairs)


def flipped(index, mask):
    result = index
    bit = 1
    while bit <= mask:
        if mask & bit:
            result = result + bit * (1 - 2 * (lax.div(index, bit) % 2))
        bit *= 2
    return result


def greet(devices):
    barrier = pltpu.get_barrier_semaphore()
    for device in devices:
        pl.semaphore_signal(barrier, inc=1, device_id=device, device_id_type=MESH)


def greeted(number):
    pl.semaphore_wait(pltpu.get_barrier_semaphore(), number)


def gather_and_iterate(count, m_hbm, g_hbm, partner_hbm, update, case, m_v, g_v, stage, arrived, x, gram, gram_low, poly,
                       partner, partner_sem, load_sem, send_sem, recv_sem):
    rep, me = lax.axis_index("rep"), lax.axis_index("fsdp")
    rows, cols = m_v.shape[1:]
    row_count = rows * count
    block = rows if rows % 128 == 0 else 256
    by_block = block == rows
    peer = [flipped(me, d) for d in range(count)]
    order = list(range(count - 1, -1, -1))

    loads = {}
    for d in order:
        loads[d] = [
            pltpu.make_async_copy(m_hbm.at[peer[d]], m_v.at[peer[d]], load_sem.at[0, d]),
            pltpu.make_async_copy(g_hbm.at[peer[d]], g_v.at[peer[d]], load_sem.at[1, d]),
        ]
        for copy in loads[d]:
            copy.start()
    partner_load = pltpu.make_async_copy(partner_hbm, partner, partner_sem)
    partner_load.start()
    greet([(rep, peer[d]) for d in range(1, count)])

    sent = {}
    for d in order:
        for copy in loads[d]:
            copy.wait()
        blended = beta_moment * m_v[peer[d]].astype(F32) + g_v[peer[d]].astype(F32)
        if d == order[0]:
            greeted(count - 1)
        if d:
            stage[d] = blended.astype(BF16)
            sent[d] = pltpu.make_async_remote_copy(
                src_ref=stage.at[d], dst_ref=arrived.at[me], send_sem=send_sem.at[d], recv_sem=recv_sem.at[d],
                device_id=(rep, peer[d]), device_id_type=MESH)
            sent[d].start()
        else:
            arrived[me] = blended.astype(BF16)

    partner_load.wait()
    last = partner_hbm.shape[0] - 1
    case[0] = 3 * lax.div(partner[0], 2) + lax.div(last - partner[last], 2)

    total = jnp.zeros((1, 1), F32)
    for d in range(count):
        if d:
            sent[d].wait_recv()
        wide = arrived[peer[d]].astype(F32)
        total = total + jnp.sum(wide * wide, axis=(0, 1), keepdims=True)
        if by_block:
            place = pl.ds(pl.multiple_of(peer[d] * rows, rows), rows)
            x[:, place] = jnp.swapaxes(arrived[peer[d]], 0, 1)
    if not by_block:
        whole = arrived[...].reshape(row_count, cols)
        for start in range(0, row_count, block):
            x[:, start : start + block] = jnp.swapaxes(whole[start : start + block], 0, 1)
    inverse = 1.0 / (jnp.sqrt(total) + epsilon_norm)
    x[...] = (x[...].astype(F32) * inverse).astype(BF16)

    half = cols // 2

    def make_poly():
        for top in (0, half):
            part = lax.dot_general(x[top : top + half, :], x[...], (((1,), (1,)), ((), ())), preferred_element_type=F32)
            gram[top : top + half, :] = part
            gram_low[top : top + half, :] = part.astype(BF16)
        for top in (0, half):
            square = jnp.dot(gram_low[top : top + half, :], gram_low[...], preferred_element_type=F32)
            poly[top : top + half, :] = (coef_second * gram[top : top + half, :] + coef_third * square).astype(BF16)

    def next_block(place):
        old = x[:, place]
        product = jnp.dot(poly[...], old, preferred_element_type=F32)
        return (coef_first * old.astype(F32) + product).astype(BF16)

    @pl.loop(0, ITERS - 1)
    def _(step):
        make_poly()
        for start in range(0, row_count, 256):
            place = slice(start, start + 256)
            x[:, place] = next_block(place)

    make_poly()
    for start in range(0, row_count, block):
        piece = jnp.swapaxes(next_block(slice(start, start + block)), 0, 1)
        update[start // rows : (start + block) // rows] = piece.reshape(block // rows, rows, cols)
    for d in range(1, count):
        sent[d].wait_send()


def return_and_average(count, masks, update, w_hbm, averaged, w_v, update_in, stepped, received, load_sem, send_sem,
                       recv_sem):
    rep, me = lax.axis_index("rep"), lax.axis_index("fsdp")
    rows = w_v.shape[1]
    peer = [flipped(me, d) for d in range(count)]
    loads = [pltpu.make_async_copy(w_hbm.at[peer[d]], w_v.at[peer[d]], load_sem.at[d]) for d in range(count)]
    for copy in loads:
        copy.start()
    known = [(rep, peer[d]) for d in range(1, count)]
    if masks is not None:
        first, last = masks
        if first == last:
            mate = flipped(rep, first)
        else:
            side = lax.div(rep, 7 - first - last) % 2
            mate = flipped(rep, first) * (1 - side) + flipped(rep, last) * side
        known.append((mate, me))
    greet(known)
    greeted(len(known))

    returns = {}
    for d in range(count - 1, 0, -1):
        returns[d] = pltpu.make_async_remote_copy(
            src_ref=update.at[peer[d]], dst_ref=update_in.at[me], send_sem=send_sem.at[0, d],
            recv_sem=recv_sem.at[0, d], device_id=(rep, peer[d]), device_id_type=MESH)
        returns[d].start()

    scale = learn_rate * 0.2 * math.sqrt(rows * count)
    passed = []
    for d in range(count):
        loads[d].wait()
        if d:
            returns[d].wait_recv()
            part = update_in[peer[d]]
        else:
            part = update[me]
        stepped[peer[d]] = (
            w_v[peer[d]].astype(F32) * (1.0 - learn_rate * decay_rate) - scale * part.astype(F32)
        ).astype(BF16)
        if masks is not None:
            copy = pltpu.make_async_remote_copy(
                src_ref=stepped.at[peer[d]], dst_ref=received.at[peer[d]], send_sem=send_sem.at[1, d],
                recv_sem=recv_sem.at[1, d], device_id=(mate, me), device_id_type=MESH)
            copy.start()
            passed.append(copy)
    if masks is None:
        averaged[...] = stepped[...]
    for d, copy in enumerate(passed):
        copy.wait_recv()
        averaged[peer[d]] = ((stepped[peer[d]].astype(F32) + received[peer[d]].astype(F32)) * 0.5).astype(BF16)
    for copy in list(returns.values()) + passed:
        copy.wait_send()


def params(number, limit):
    return pltpu.CompilerParams(collective_id=number, has_side_effects=True, vmem_limit_bytes=limit * 1024 * 1024)


def orthogonalized(number, momentum, gradient, partner):
    count = lax.axis_size("fsdp")
    _, _, rows, cols = momentum.shape
    tile = pltpu.VMEM((count, rows, cols), BF16)
    square = (cols, cols)
    return pl.pallas_call(
        functools.partial(gather_and_iterate, count),
        out_shape=[jax.ShapeDtypeStruct((count, rows, cols), BF16), jax.ShapeDtypeStruct((1,), jnp.int32)],
        in_specs=[pl.BlockSpec(memory_space=pltpu.HBM)] * 3,
        out_specs=[pl.BlockSpec(memory_space=pltpu.VMEM), pl.BlockSpec(memory_space=pltpu.SMEM)],
        scratch_shapes=[tile] * 4
        + [pltpu.VMEM((cols, rows * count), BF16), pltpu.VMEM(square, F32)]
        + [pltpu.VMEM(square, BF16)] * 2
        + [pltpu.SMEM(partner.shape, jnp.int32), pltpu.SemaphoreType.DMA]
        + [pltpu.SemaphoreType.DMA((2, count)), pltpu.SemaphoreType.DMA((count,)), pltpu.SemaphoreType.DMA((count,))],
        compiler_params=params(number, 60),
    )(momentum[0], gradient[0], partner)


def finished(masks, number, update, weights):
    count = lax.axis_size("fsdp")
    tile = pltpu.VMEM(weights.shape[1:], BF16)
    return pl.pallas_call(
        functools.partial(return_and_average, count, masks),
        out_shape=jax.ShapeDtypeStruct(weights.shape[1:], BF16),
        in_specs=[pl.BlockSpec(memory_space=pltpu.VMEM), pl.BlockSpec(memory_space=pltpu.HBM)],
        out_specs=pl.BlockSpec(memory_space=pltpu.VMEM),
        scratch_shapes=[tile] * 4
        + [pltpu.SemaphoreType.DMA((count,))]
        + [pltpu.SemaphoreType.DMA((2, count))] * 2,
        compiler_params=params(number, 24),
    )(update, weights[0])


def averaged_by_permutes(stepped, partner):
    rep_count = lax.axis_size("rep")
    own_index = lax.axis_index("rep")
    differ = jnp.bitwise_xor(partner[own_index], own_index)
    received = jnp.zeros_like(stepped)
    for bit_number in range(rep_count.bit_length() - 1):
        other = swapped(stepped, "rep", bit_number)
        received = jnp.where(differ == 1 << bit_number, other, received)
    return ((stepped.astype(F32) + received.astype(F32)) * 0.5).astype(BF16)


def local(weights, momentum, gradient, partner):
    update, case = orthogonalized(0, momentum, gradient, partner)
    if lax.axis_size("rep") != 8:
        return averaged_by_permutes(finished(None, 1, update, weights)[None], partner)
    branches = [
        functools.partial(finished, (first, last), 1 + 3 * row + column)
        for row, first in enumerate((1, 2, 4))
        for column, last in enumerate((1, 2, 4))
    ]
    return lax.switch(case[0], branches, update, weights)[None]


def solution(mesh):
    spec = P("rep", None, "fsdp", None)
    return jax.shard_map(local, mesh=mesh, in_specs=(spec, spec, spec, P()), out_specs=spec, check_vma=False)
```

profile of v0, /device:TPU:0, one launch (start us, length us, event | category | flops | bytes accessed | tf_op | source)
XLA Modules:
  0.0 55.5 jit_solution(12748771181199834058)
XLA Ops:
  0.0 0.0 copy-start
  0.0 25.9 %shard_map.55 = (bf16[4,256,512]{2,1,0:T(8,128)(2,1)S(1)}, s32[1]{0:T(128)}) custom-call(bf16[4,256,512]{2,1,0:T(8,128)(2,1)} %bitcast.39, bf16[4,256,512]{2,1,0:T(8,128)(2,1)} %bitcast.40, s32[8]{0:T(128)} %partner_hbm.1), custom_call_target="tpu_custom_call" | custom-call | tf_op jit(solution)/shard_map/pallas_call | solution.py:203
  26.5 0.0 copy-done
  26.5 28.0 %conditional.1 = (bf16[1,4,256,512]{3,2,1,0:T(8,128)(2,1)S(1)}) conditional(s32[]{:T(128)} %bitcast.20, (bf16[1,4,256,512]{3,2,1,0:T(8,128)(2,1)S(1)}, bf16[4,256,512]{2,1,0:T(8,128)(2,1)S(1)}) %tuple.60, (bf16[1,4,256,512]{3,2,1,0:T(8,128)(2,1)S(1)}, bf16[4,256,512]{2,1,0:T(8,128)(2,1)S(1)}) %tuple.61, ...), branch_computations={%region_0.0_spmd, %region_1.0_spmd, %region_2.0_spmd, %region_3.0_... | conditional | bytes 8 | solution.py:252
  26.6 28.0 %branch_2_fun.1 = bf16[4,256,512]{2,1,0:T(8,128)(2,1)S(1)} custom-call(bf16[4,256,512]{2,1,0:T(8,128)(2,1)S(1)} %get-tuple-element.54.update, bf16[4,256,512]{2,1,0:T(8,128)(2,1)S(1)} %bitcast.23), custom_call_target="tpu_custom_call" | custom-call | tf_op jit(solution)/shard_map/cond/branch_2_fun/pallas_call | solution.py:220
  54.6 1.0 %copy.24 = bf16[1,4,256,512]{3,2,1,0:T(8,128)(2,1)} copy(bf16[1,4,256,512]{3,2,1,0:T(8,128)(2,1)S(1)} %get-tuple-element.74) | data formatting | bytes 2097152
Async XLA Ops:
  0.0 26.5 %copy-start = (bf16[1,4,256,512]{3,2,1,0:T(8,128)(2,1)S(1)}, bf16[1,4,256,512]{3,2,1,0:T(8,128)(2,1)}, u32[]{:S(2)}) copy-start(bf16[1,4,256,512]{3,2,1,0:T(8,128)(2,1)} %param.13) | copy-start | bytes 3145732
where the time goes:
time: 56.2 us; the launch traced here: 55.5 us
  Pallas kernels  53.9 us (96%)
  local copies, waits for them, and re-layouts  0.98 us (2%)
  between operations  0.65 us (1%)
    pallas_call x1, Pallas kernels, finished(): pl.pallas_call(functools.partial(return_and_average, count, masks), out_s...  28 us
    pallas_call x1, Pallas kernels, orthogonalized(): pl.pallas_call(functools.partial(gather_and_iterate, count), out_shape=[j...  25.9 us

commit v1 on v0

--- a/solution.py
+++ b/solution.py
@@ -36,6 +36,14 @@
             result = result + bit * (1 - 2 * (lax.div(index, bit) % 2))
         bit *= 2
     return result
+
+
+PIECES = 2
+
+
+def pieces(rows):
+    length = rows // PIECES if rows % (PIECES * 128) == 0 else rows
+    return [pl.ds(start, length) for start in range(0, rows, length)]
 
 
 def greet(devices):
@@ -58,47 +66,51 @@
     peer = [flipped(me, d) for d in range(count)]
     order = list(range(count - 1, -1, -1))
 
+    parts = pieces(rows)
     loads = {}
     for d in order:
-        loads[d] = [
-            pltpu.make_async_copy(m_hbm.at[peer[d]], m_v.at[peer[d]], load_sem.at[0, d]),
-            pltpu.make_async_copy(g_hbm.at[peer[d]], g_v.at[peer[d]], load_sem.at[1, d]),
-        ]
-        for copy in loads[d]:
-            copy.start()
+        for number, part in enumerate(parts):
+            loads[d, number] = [
+                pltpu.make_async_copy(m_hbm.at[peer[d], part], m_v.at[peer[d], part], load_sem.at[0, d, number]),
+                pltpu.make_async_copy(g_hbm.at[peer[d], part], g_v.at[peer[d], part], load_sem.at[1, d, number]),
+            ]
+            for copy in loads[d, number]:
+                copy.start()
     partner_load = pltpu.make_async_copy(partner_hbm, partner, partner_sem)
     partner_load.start()
     greet([(rep, peer[d]) for d in range(1, count)])
 
     sent = {}
     for d in order:
-        for copy in loads[d]:
-            copy.wait()
-        blended = beta_moment * m_v[peer[d]].astype(F32) + g_v[peer[d]].astype(F32)
-        if d == order[0]:
-            greeted(count - 1)
-        if d:
-            stage[d] = blended.astype(BF16)
-            sent[d] = pltpu.make_async_remote_copy(
-                src_ref=stage.at[d], dst_ref=arrived.at[me], send_sem=send_sem.at[d], recv_sem=recv_sem.at[d],
-                device_id=(rep, peer[d]), device_id_type=MESH)
-            sent[d].start()
-        else:
-            arrived[me] = blended.astype(BF16)
+        for number, part in enumerate(parts):
+            for copy in loads[d, number]:
+                copy.wait()
+            blended = beta_moment * m_v[peer[d], part].astype(F32) + g_v[peer[d], part].astype(F32)
+            if d:
+                stage[d, part] = blended.astype(BF16)
+                if d == order[0] and number == 0:
+                    greeted(count - 1)
+                sent[d, number] = pltpu.make_async_remote_copy(
+                    src_ref=stage.at[d, part], dst_ref=arrived.at[me, part], send_sem=send_sem.at[d, number],
+                    recv_sem=recv_sem.at[d, number], device_id=(rep, peer[d]), device_id_type=MESH)
+                sent[d, number].start()
+            else:
+                arrived[me, part] = blended.astype(BF16)
 
     partner_load.wait()
     last = partner_hbm.shape[0] - 1
     case[0] = 3 * lax.div(partner[0], 2) + lax.div(last - partner[last], 2)
 
     total = jnp.zeros((1, 1), F32)
-    for d in range(count):
-        if d:
-            sent[d].wait_recv()
-        wide = arrived[peer[d]].astype(F32)
-        total = total + jnp.sum(wide * wide, axis=(0, 1), keepdims=True)
-        if by_block:
-            place = pl.ds(pl.multiple_of(peer[d] * rows, rows), rows)
-            x[:, place] = jnp.swapaxes(arrived[peer[d]], 0, 1)
+    for d in [0, 1] + list(range(count - 1, 1, -1)):
+        for number, part in enumerate(parts):
+            if d:
+                sent[d, number].wait_recv()
+            wide = arrived[peer[d], part].astype(F32)
+            total = total + jnp.sum(wide * wide, axis=(0, 1), keepdims=True)
+            if by_block:
+                place = pl.ds(pl.multiple_of(peer[d] * rows + part.start, part.size), part.size)
+                x[:, place] = jnp.swapaxes(arrived[peer[d], part], 0, 1)
     if not by_block:
         whole = arrived[...].reshape(row_count, cols)
         for start in range(0, row_count, block):
@@ -109,21 +121,32 @@
     half = cols // 2
 
     def make_poly():
-        for top in (0, half):
-            part = lax.dot_general(x[top : top + half, :], x[...], (((1,), (1,)), ((), ())), preferred_element_type=F32)
-            gram[top : top + half, :] = part
-            gram_low[top : top + half, :] = part.astype(BF16)
-        for top in (0, half):
-            square = jnp.dot(gram_low[top : top + half, :], gram_low[...], preferred_element_type=F32)
-            poly[top : top + half, :] = (coef_second * gram[top : top + half, :] + coef_third * square).astype(BF16)
+        left, right = slice(0, half), slice(half, cols)
+
+        def outer(first, second):
+            return lax.dot_general(
+                x[first, :], x[second, :], (((1,), (1,)), ((), ())), preferred_element_type=F32
+            )
+
+        for first, second in ((left, left), (left, right), (right, right)):
+            part = outer(first, second)
+            gram[first, second] = part
+            gram_low[first, second] = part.astype(BF16)
+            if first != second:
+                gram_low[second, first] = jnp.swapaxes(part.astype(BF16), 0, 1)
+        for first, second in ((left, left), (left, right), (right, right)):
+            square = jnp.dot(gram_low[first, :], gram_low[:, second], preferred_element_type=F32)
+            part = (coef_second * gram[first, second] + coef_third * square).astype(BF16)
+            poly[first, second] = part
+            if first != second:
+                poly[second, first] = jnp.swapaxes(part, 0, 1)
 
     def next_block(place):
         old = x[:, place]
         product = jnp.dot(poly[...], old, preferred_element_type=F32)
         return (coef_first * old.astype(F32) + product).astype(BF16)
 
-    @pl.loop(0, ITERS - 1)
-    def _(step):
+    for step in range(ITERS - 1):
         make_poly()
         for start in range(0, row_count, 256):
             place = slice(start, start + 256)
@@ -133,8 +156,8 @@
     for start in range(0, row_count, block):
         piece = jnp.swapaxes(next_block(slice(start, start + block)), 0, 1)
         update[start // rows : (start + block) // rows] = piece.reshape(block // rows, rows, cols)
-    for d in range(1, count):
-        sent[d].wait_send()
+    for copy in sent.values():
+        copy.wait_send()
 
 
 def return_and_average(count, masks, update, w_hbm, averaged, w_v, update_in, stepped, received, load_sem, send_sem,
@@ -142,9 +165,15 @@
     rep, me = lax.axis_index("rep"), lax.axis_index("fsdp")
     rows = w_v.shape[1]
     peer = [flipped(me, d) for d in range(count)]
-    loads = [pltpu.make_async_copy(w_hbm.at[peer[d]], w_v.at[peer[d]], load_sem.at[d]) for d in range(count)]
-    for copy in loads:
-        copy.start()
+    taken = [0, 1] + list(range(count - 1, 1, -1))
+    parts = [pl.ds(0, rows)]
+    every = [(d, number, part) for d in taken for number, part in enumerate(parts)]
+    loads = {}
+    for d, number, part in every:
+        loads[d, number] = pltpu.make_async_copy(
+            w_hbm.at[peer[d], part], w_v.at[peer[d], part], load_sem.at[d, number]
+        )
+        loads[d, number].start()
     known = [(rep, peer[d]) for d in range(1, count)]
     if masks is not None:
         first, last = masks
@@ -159,35 +188,39 @@
 
     returns = {}
     for d in range(count - 1, 0, -1):
-        returns[d] = pltpu.make_async_remote_copy(
-            src_ref=update.at[peer[d]], dst_ref=update_in.at[me], send_sem=send_sem.at[0, d],
-            recv_sem=recv_sem.at[0, d], device_id=(rep, peer[d]), device_id_type=MESH)
-        returns[d].start()
+        for number, part in enumerate(parts):
+            returns[d, number] = pltpu.make_async_remote_copy(
+                src_ref=update.at[peer[d], part], dst_ref=update_in.at[me, part], send_sem=send_sem.at[0, d, number],
+                recv_sem=recv_sem.at[0, d, number], device_id=(rep, peer[d]), device_id_type=MESH)
+            returns[d, number].start()
 
     scale = learn_rate * 0.2 * math.sqrt(rows * count)
-    passed = []
-    for d in range(count):
-        loads[d].wait()
+    passed = {}
+    for d, number, part in every:
+        loads[d, number].wait()
         if d:
-            returns[d].wait_recv()
-            part = update_in[peer[d]]
+            returns[d, number].wait_recv()
+            change = update_in[peer[d], part]
         else:
-            part = update[me]
-        stepped[peer[d]] = (
-            w_v[peer[d]].astype(F32) * (1.0 - learn_rate * decay_rate) - scale * part.astype(F32)
+            change = update[me, part]
+        stepped[peer[d], part] = (
+            w_v[peer[d], part].astype(F32) * (1.0 - learn_rate * decay_rate) - scale * change.astype(F32)
         ).astype(BF16)
         if masks is not None:
-            copy = pltpu.make_async_remote_copy(
-                src_ref=stepped.at[peer[d]], dst_ref=received.at[peer[d]], send_sem=send_sem.at[1, d],
-                recv_sem=recv_sem.at[1, d], device_id=(mate, me), device_id_type=MESH)
-            copy.start()
-            passed.append(copy)
+            passed[d, number] = pltpu.make_async_remote_copy(
+                src_ref=stepped.at[peer[d], part], dst_ref=received.at[peer[d], part],
+                send_sem=send_sem.at[1, d, number], recv_sem=recv_sem.at[1, d, number],
+                device_id=(mate, me), device_id_type=MESH)
+            passed[d, number].start()
     if masks is None:
         averaged[...] = stepped[...]
-    for d, copy in enumerate(passed):
-        copy.wait_recv()
-        averaged[peer[d]] = ((stepped[peer[d]].astype(F32) + received[peer[d]].astype(F32)) * 0.5).astype(BF16)
-    for copy in list(returns.values()) + passed:
+    else:
+        for d, number, part in every:
+            passed[d, number].wait_recv()
+            averaged[peer[d], part] = (
+                (stepped[peer[d], part].astype(F32) + received[peer[d], part].astype(F32)) * 0.5
+            ).astype(BF16)
+    for copy in list(returns.values()) + list(passed.values()):
         copy.wait_send()
 
 
@@ -209,7 +242,8 @@
         + [pltpu.VMEM((cols, rows * count), BF16), pltpu.VMEM(square, F32)]
         + [pltpu.VMEM(square, BF16)] * 2
         + [pltpu.SMEM(partner.shape, jnp.int32), pltpu.SemaphoreType.DMA]
-        + [pltpu.SemaphoreType.DMA((2, count)), pltpu.SemaphoreType.DMA((count,)), pltpu.SemaphoreType.DMA((count,))],
+        + [pltpu.SemaphoreType.DMA((2, count, PIECES))]
+        + [pltpu.SemaphoreType.DMA((count, PIECES))] * 2,
         compiler_params=params(number, 60),
     )(momentum[0], gradient[0], partner)
 
@@ -223,8 +257,8 @@
         in_specs=[pl.BlockSpec(memory_space=pltpu.VMEM), pl.BlockSpec(memory_space=pltpu.HBM)],
         out_specs=pl.BlockSpec(memory_space=pltpu.VMEM),
         scratch_shapes=[tile] * 4
-        + [pltpu.SemaphoreType.DMA((count,))]
-        + [pltpu.SemaphoreType.DMA((2, count))] * 2,
+        + [pltpu.SemaphoreType.DMA((count, 1))]
+        + [pltpu.SemaphoreType.DMA((2, count, 1))] * 2,
         compiler_params=params(number, 24),
     )(update, weights[0])
 

time: 56.2 us -> 53.2 us (0.947); the launches traced: 55.5 us -> 53.2 us
  Pallas kernels: 53.9 us -> 51.1 us
    pallas_call x1, Pallas kernels: 25.9 us -> 24.3 us  [orthogonalized(): pl.pallas_call(functools.partial(gather_and_iterate, count), out_shape=[j...]
    pallas_call x1, Pallas kernels: 28 us -> 26.8 us  [finished(): pl.pallas_call(functools.partial(return_and_average, count, masks), out_s...]
where the time goes in v1:
time: 53.2 us
  Pallas kernels  51.1 us (96%)
  local copies, waits for them, and re-layouts  0.98 us (2%)
  between operations  0.65 us (1%)
    pallas_call x1, Pallas kernels, finished(): pl.pallas_call(functools.partial(return_and_average, count, masks), out_s...  26.8 us
    pallas_call x1, Pallas kernels, orthogonalized(): pl.pallas_call(functools.partial(gather_and_iterate, count), out_shape=[j...  24.3 us

profile of v1, /device:TPU:0, one launch (start us, length us, event | category | flops | bytes accessed | tf_op | source)
XLA Modules:
  0.0 53.2 jit_solution(15965693178089896098)
XLA Ops:
  0.0 0.0 copy-start
  0.0 24.3 %shard_map.55 = (bf16[4,256,512]{2,1,0:T(8,128)(2,1)S(1)}, s32[1]{0:T(128)}) custom-call(bf16[4,256,512]{2,1,0:T(8,128)(2,1)} %bitcast.39, bf16[4,256,512]{2,1,0:T(8,128)(2,1)} %bitcast.40, s32[8]{0:T(128)} %partner_hbm.1), custom_call_target="tpu_custom_call" | custom-call | tf_op jit(solution)/shard_map/pallas_call | solution.py:236
  24.9 0.0 copy-done
  24.9 27.2 %conditional.1 = (bf16[1,4,256,512]{3,2,1,0:T(8,128)(2,1)S(1)}) conditional(s32[]{:T(128)} %bitcast.20, (bf16[1,4,256,512]{3,2,1,0:T(8,128)(2,1)S(1)}, bf16[4,256,512]{2,1,0:T(8,128)(2,1)S(1)}) %tuple.60, (bf16[1,4,256,512]{3,2,1,0:T(8,128)(2,1)S(1)}, bf16[4,256,512]{2,1,0:T(8,128)(2,1)S(1)}) %tuple.61, ...), branch_computations={%region_0.0_spmd, %region_1.0_spmd, %region_2.0_spmd, %region_3.0_... | conditional | bytes 8 | solution.py:286
  25.0 26.8 %branch_4_fun.1 = bf16[4,256,512]{2,1,0:T(8,128)(2,1)S(1)} custom-call(bf16[4,256,512]{2,1,0:T(8,128)(2,1)S(1)} %get-tuple-element.60.update, bf16[4,256,512]{2,1,0:T(8,128)(2,1)S(1)} %bitcast.25), custom_call_target="tpu_custom_call" | custom-call | tf_op jit(solution)/shard_map/cond/branch_4_fun/pallas_call | solution.py:254
  52.2 1.0 %copy.24 = bf16[1,4,256,512]{3,2,1,0:T(8,128)(2,1)} copy(bf16[1,4,256,512]{3,2,1,0:T(8,128)(2,1)S(1)} %get-tuple-element.74) | data formatting | bytes 2097152
Async XLA Ops:
  0.0 24.9 %copy-start = (bf16[1,4,256,512]{3,2,1,0:T(8,128)(2,1)S(1)}, bf16[1,4,256,512]{3,2,1,0:T(8,128)(2,1)}, u32[]{:S(2)}) copy-start(bf16[1,4,256,512]{3,2,1,0:T(8,128)(2,1)} %param.13) | copy-start | bytes 3145732
